TPU v7x, 32 devices: a whole 2x2x4 slice. The times are simulated.
32 devices in a mesh: sfc: 32 (over z, y, x, core).
Axes of the slice: x: 2, y: 2, z: 4, core: 2. Of those that a mesh axis runs over, the one named last changes fastest.
Arguments:
- rhs: float32 [4, 4, 4, 4096], P(None, None, None, 'sfc'), may hold values from -6 to 6
- screen: float32 [4, 4, 4, 4096], P(None, None, None, 'sfc'), may hold values from 0.05 to 2
- guess: float32 [4, 4, 4, 4096], P(None, None, None, 'sfc'), may hold values from -3 to 3
- counts: int32 [32], replicated, may hold values from 32 to 128, as said below
- neighbours: int32 [6, 4096], P(None, 'sfc'), may hold values from -1 to 263, as said below
Outputs:
- solution: float32 [4, 4, 4, 4096], P(None, None, None, 'sfc')
Inputs may be any that keep to these rules, and one draw needn't show every extreme that they name: `counts`: each count is a multiple of 8; one device holds 128 live blocks and another 128 // 4. `neighbours`: A code (d + 1) * 128 + s names slot s of the device d places further along, d in -1, 0, 1, always a live slot; a block on the previous device is among its last 8 live slots and then the naming block is among the first 8 slots, a block on the next device is among its first 8 slots and then the naming block is among the last 8 live slots; dead slots name none.
All inputs are finite; a program needn't handle non-finite values.
Results may differ from a plain program's by a relative error of at most 0.0001.
Values sent between devices are 32-bit elements; how exact they have to be, the bound alone decides.
A program may use at most 64 MiB of HBM per device.

v0:
```python
import jax
import jax.numpy as jnp
from jax import lax
from jax.sharding import PartitionSpec as P

SWEEPS = 2


OMEGA = 0.8
COARSE = 8.0


def padded(value, sides, width):
    for axis, dim in sides:
        size, length = (lax.axis_size(axis), value.shape[dim])
        up = [(i, (i + 1) % size) for i in range(size - 1)]
        down = [(j, i) for i, j in up]
        last = lax.slice_in_dim(value, length - width, length, axis=dim)
        leading = lax.slice_in_dim(value, 0, width, axis=dim)
        before = lax.ppermute(last, axis, up)
        after = lax.ppermute(leading, axis, down)
        value = jnp.concatenate([before, value, after], axis=dim)
    return value


def partner(value, axis, distance):
    mask = 2**distance
    pairs = [(source, source ^ mask) for source in range(lax.axis_size(axis))]
    return lax.ppermute(value, axis, pairs)


def lower_pad(values, face, along):
    edge_count = values.shape[along]
    return jnp.concatenate(
        [face, lax.slice_in_dim(values, 0, edge_count - 1, axis=along)], axis=along
    )


def upper_pad(values, face, along):
    edge_count = values.shape[along]
    return jnp.concatenate([lax.slice_in_dim(values, 1, edge_count, axis=along), face], axis=along)


def neighbour_total(values, source, columns):
    total = jnp.zeros_like(values)
    for along in range(3):
        edge_count = values.shape[along]
        for upward in range(2):
            column = columns[2 * along + upward]
            valid = (column >= 0).astype(jnp.float32)
            safe = jnp.where(column >= 0, column, 0)
            edge = edge_count - 1 if upward == 0 else 0
            face = lax.slice_in_dim(source, edge, edge + 1, axis=along)
            face = jnp.take(face, safe, axis=3) * valid
            if upward == 0:
                total = total + lower_pad(values, face, along)
            else:
                total = total + upper_pad(values, face, along)
    return total


def restrict(values):
    half = values.shape[0] // 2
    width = values.shape[3]
    return values.reshape(half, 2, half, 2, half, 2, width).sum(axis=(1, 3, 5)) * 0.5


def prolong(values):
    return jnp.repeat(jnp.repeat(jnp.repeat(values, 2, axis=0), 2, axis=1), 2, axis=2)


def per_device(rhs, screen, guess, counts, neighbours):
    slot_count = rhs.shape[3]
    devices = lax.axis_size("sfc")
    rank = lax.axis_index("sfc")
    own_live = lax.dynamic_index_in_dim(counts, rank, keepdims=False)
    live = jnp.arange(slot_count, dtype=jnp.int32) < own_live
    columns = jnp.where(neighbours >= 0, neighbours, -1)

    def extended(values):
        return padded(values, (("sfc", 3),), slot_count)

    def apply_operator(values, screening):
        return (6.0 + screening) * values - neighbour_total(values, extended(values), columns)

    def relax(values, forcing, screening):
        defect = forcing - apply_operator(values, screening)
        return jnp.where(live, values + OMEGA * defect / (6.0 + screening), 0.0)

    forcings = [jnp.where(live, rhs, 0.0)]
    screens = [jnp.where(live, screen, 0.0)]
    current = jnp.where(live, guess, 0.0)
    kept = []
    defect = None
    for depth in range(3):
        for sweep_index in range(SWEEPS):
            if depth > 0 and sweep_index == 0:
                current = jnp.where(live, OMEGA * forcings[depth] / (6.0 + screens[depth]), 0.0)
            else:
                current = relax(current, forcings[depth], screens[depth])
        kept.append(current)
        defect = jnp.where(live, forcings[depth] - apply_operator(current, screens[depth]), 0.0)
        if depth < 2:
            forcings.append(restrict(defect))
            screens.append(restrict(screens[depth]))
            current = jnp.zeros_like(forcings[depth + 1])
    grouped = defect.reshape(slot_count // 8, 8).sum(axis=1) * 0.5
    levels_coarse = devices.bit_length() - 1
    running = grouped
    correction = grouped / COARSE
    for bit_index in range(levels_coarse):
        running = running + partner(running, "sfc", bit_index)
        correction = correction + running / (COARSE * 2 ** (bit_index + 1))
    spread = jnp.repeat(correction, 8).reshape(1, 1, 1, slot_count)
    current = kept[2] + jnp.where(live, spread, 0.0)
    for depth in (2, 1, 0):
        if depth < 2:
            current = kept[depth] + jnp.where(live, prolong(current), 0.0)
        for sweep_index in range(SWEEPS):
            current = relax(current, forcings[depth], screens[depth])
    return current


def solution(mesh):
    in_specs = (
        P(None, None, None, "sfc"),
        P(None, None, None, "sfc"),
        P(None, None, None, "sfc"),
        P(),
        P(None, "sfc"),
    )
    out_specs = P(None, None, None, "sfc")
    return jax.shard_map(
        per_device, mesh=mesh, in_specs=in_specs, out_specs=out_specs, check_vma=False
    )
```

profile of v0, /device:TPU:15, one launch (start us, length us, event | category | flops | bytes accessed | tf_op | source)
XLA Modules:
  0.0 236.0 jit_solution(13103278507620803490)
XLA Ops:
  2.7 3.7 %collective-permute-start = (f32[4,4,4,128]{3,2,1,0:T(4,128)S(1)}, f32[4,4,4,128]{3,2,1,0:T(4,128)S(1)}, u32[]{:S(2)}, u32[]{:S(2)}) collective-permute-start(f32[4,4,4,128]{3,2,1,0:T(4,128)S(1)} %broadcast_select_fusion.1), channel_id=1, source_target_pairs={{0,1},{1,2},{2,3},{3,4},{4,5},{5,6},{6,7},{7,8},{8,9},{9,10},{10,1... | collective-permute-start | bytes 98312 | tf_op jit(solution)/shard_map/ppermute | solution.py:20
  6.3 1.9 collective-permute-start.1
  9.1 4.3 %collective-permute-done.1 = f32[4,4,4,128]{3,2,1,0:T(4,128)S(1)} collective-permute-done((f32[4,4,4,128]{3,2,1,0:T(4,128)S(1)}, f32[4,4,4,128]{3,2,1,0:T(4,128)S(1)}, u32[]{:S(2)}, u32[]{:S(2)}) %collective-permute-start.1) | collective-permute-done | bytes 32800 | tf_op jit(solution)/shard_map/ppermute | solution.py:21
  21.7 1.9 collective-permute-start.2
  23.7 2.4 %collective-permute-start.3 = (f32[4,4,4,128]{3,2,1,0:T(4,128)S(1)}, f32[4,4,4,128]{3,2,1,0:T(4,128)S(1)}, u32[]{:S(2)}, u32[]{:S(2)}) collective-permute-start(f32[4,4,4,128]{3,2,1,0:T(4,128)S(1)} %add_select_fusion.3), channel_id=1, source_target_pairs={{1,0},{2,1},{3,2},{4,3},{5,4},{6,5},{7,6},{8,7},{9,8},{10,9},{11,1... | collective-permute-start | bytes 98312 | tf_op jit(solution)/shard_map/ppermute | solution.py:21
  26.2 4.6 %collective-permute-done.3 = f32[4,4,4,128]{3,2,1,0:T(4,128)S(1)} collective-permute-done((f32[4,4,4,128]{3,2,1,0:T(4,128)S(1)}, f32[4,4,4,128]{3,2,1,0:T(4,128)S(1)}, u32[]{:S(2)}, u32[]{:S(2)}) %collective-permute-start.3) | collective-permute-done | bytes 32800 | tf_op jit(solution)/shard_map/ppermute | solution.py:21
  38.3 1.9 collective-permute-start.4
  40.3 2.4 %collective-permute-start.5 = (f32[4,4,4,128]{3,2,1,0:T(4,128)S(1)}, f32[4,4,4,128]{3,2,1,0:T(4,128)S(1)}, u32[]{:S(2)}, u32[]{:S(2)}) collective-permute-start(f32[4,4,4,128]{3,2,1,0:T(4,128)S(1)} %add_select_fusion.2), channel_id=1, source_target_pairs={{1,0},{2,1},{3,2},{4,3},{5,4},{6,5},{7,6},{8,7},{9,8},{10,9},{11,1... | collective-permute-start | bytes 98312 | tf_op jit(solution)/shard_map/ppermute | solution.py:21
  42.8 4.6 %collective-permute-done.5 = f32[4,4,4,128]{3,2,1,0:T(4,128)S(1)} collective-permute-done((f32[4,4,4,128]{3,2,1,0:T(4,128)S(1)}, f32[4,4,4,128]{3,2,1,0:T(4,128)S(1)}, u32[]{:S(2)}, u32[]{:S(2)}) %collective-permute-start.5) | collective-permute-done | bytes 32800 | tf_op jit(solution)/shard_map/ppermute | solution.py:21
  55.0 1.9 collective-permute-start.6
  56.9 2.6 %collective-permute-start.7 = (f32[2,2,2,128]{3,2,1,0:T(2,128)S(1)}, f32[2,2,2,128]{3,2,1,0:T(2,128)S(1)}, u32[]{:S(2)}, u32[]{:S(2)}) collective-permute-start(f32[2,2,2,128]{3,2,1,0:T(2,128)S(1)} %fusion.89), channel_id=1, source_target_pairs={{1,0},{2,1},{3,2},{4,3},{5,4},{6,5},{7,6},{8,7},{9,8},{10,9},{11,1... | collective-permute-start | bytes 12296 | tf_op jit(solution)/shard_map/ppermute | solution.py:21
  59.6 4.1 %collective-permute-done.7 = f32[2,2,2,128]{3,2,1,0:T(2,128)S(1)} collective-permute-done((f32[2,2,2,128]{3,2,1,0:T(2,128)S(1)}, f32[2,2,2,128]{3,2,1,0:T(2,128)S(1)}, u32[]{:S(2)}, u32[]{:S(2)}) %collective-permute-start.7) | collective-permute-done | bytes 4128 | tf_op jit(solution)/shard_map/ppermute | solution.py:21
  70.2 1.9 collective-permute-start.8
  72.2 2.4 %collective-permute-start.9 = (f32[2,2,2,128]{3,2,1,0:T(2,128)S(1)}, f32[2,2,2,128]{3,2,1,0:T(2,128)S(1)}, u32[]{:S(2)}, u32[]{:S(2)}) collective-permute-start(f32[2,2,2,128]{3,2,1,0:T(2,128)S(1)} %add_select_fusion.6), channel_id=1, source_target_pairs={{1,0},{2,1},{3,2},{4,3},{5,4},{6,5},{7,6},{8,7},{9,8},{10,9},{11,1... | collective-permute-start | bytes 12296 | tf_op jit(solution)/shard_map/ppermute | solution.py:21
  74.6 4.3 %collective-permute-done.9 = f32[2,2,2,128]{3,2,1,0:T(2,128)S(1)} collective-permute-done((f32[2,2,2,128]{3,2,1,0:T(2,128)S(1)}, f32[2,2,2,128]{3,2,1,0:T(2,128)S(1)}, u32[]{:S(2)}, u32[]{:S(2)}) %collective-permute-start.9) | collective-permute-done | bytes 4128 | tf_op jit(solution)/shard_map/ppermute | solution.py:21
  86.1 1.9 collective-permute-start.10
  88.1 2.4 %collective-permute-start.11 = (f32[1,1,1,128]{3,2,1,0:T(1,128)S(1)}, f32[1,1,1,128]{3,2,1,0:T(1,128)S(1)}, u32[]{:S(2)}, u32[]{:S(2)}) collective-permute-start(f32[1,1,1,128]{3,2,1,0:T(1,128)S(1)} %fusion.146), channel_id=1, source_target_pairs={{1,0},{2,1},{3,2},{4,3},{5,4},{6,5},{7,6},{8,7},{9,8},{10,9},{11,1... | collective-permute-start | bytes 1544 | tf_op jit(solution)/shard_map/ppermute | solution.py:21
  90.5 4.3 %collective-permute-done.11 = f32[1,1,1,128]{3,2,1,0:T(1,128)S(1)} collective-permute-done((f32[1,1,1,128]{3,2,1,0:T(1,128)S(1)}, f32[1,1,1,128]{3,2,1,0:T(1,128)S(1)}, u32[]{:S(2)}, u32[]{:S(2)}) %collective-permute-start.11) | collective-permute-done | bytes 544 | tf_op jit(solution)/shard_map/ppermute | solution.py:21
  96.0 1.3 gather_fusion.31
  98.6 1.3 gather_fusion.33
  101.1 1.3 gather_fusion.35
  103.1 2.0 collective-permute-start.12
  105.1 2.3 collective-permute-start.13
  107.4 4.3 %collective-permute-done.13 = f32[1,1,1,128]{3,2,1,0:T(1,128)S(1)} collective-permute-done((f32[1,1,1,128]{3,2,1,0:T(1,128)S(1)}, f32[1,1,1,128]{3,2,1,0:T(1,128)S(1)}, u32[]{:S(2)}, u32[]{:S(2)}) %collective-permute-start.13) | collective-permute-done | bytes 544 | tf_op jit(solution)/shard_map/ppermute | solution.py:21
  114.3 1.3 gather_fusion.38
  116.8 1.3 gather_fusion.40
  121.5 2.4 %collective-permute-done.15 = f32[16]{0:T(128)S(1)} collective-permute-done((f32[16]{0:T(128)S(1)}, f32[16]{0:T(128)S(1)}, u32[]{:S(2)}, u32[]{:S(2)}) %collective-permute-start.15) | collective-permute-done | bytes 96 | tf_op jit(solution)/shard_map/ppermute | solution.py:29
  123.9 2.4 %collective-permute-done.16 = f32[16]{0:T(128)S(1)} collective-permute-done((f32[16]{0:T(128)S(1)}, f32[16]{0:T(128)S(1)}, u32[]{:S(2)}, u32[]{:S(2)}) %collective-permute-start.16) | collective-permute-done | bytes 96 | tf_op jit(solution)/shard_map/ppermute | solution.py:29
  126.4 2.2 collective-permute-done.17
  129.7 2.3 collective-permute-done.18
  132.8 6.8 %collective-permute-start.19 = (f32[1,1,1,128]{3,2,1,0:T(1,128)S(1)}, f32[1,1,1,128]{3,2,1,0:T(1,128)S(1)}, u32[]{:S(2)}, u32[]{:S(2)}) collective-permute-start(f32[1,1,1,128]{3,2,1,0:T(1,128)S(1)} %select_add_fusion.2), channel_id=1, source_target_pairs={{0,1},{1,2},{2,3},{3,4},{4,5},{5,6},{6,7},{7,8},{8,9},{9,10},{10,1... | collective-permute-start | bytes 1544 | tf_op jit(solution)/shard_map/ppermute | solution.py:20
  139.6 1.9 collective-permute-start.20
  141.5 4.7 %collective-permute-done.20 = f32[1,1,1,128]{3,2,1,0:T(1,128)S(1)} collective-permute-done((f32[1,1,1,128]{3,2,1,0:T(1,128)S(1)}, f32[1,1,1,128]{3,2,1,0:T(1,128)S(1)}, u32[]{:S(2)}, u32[]{:S(2)}) %collective-permute-start.20) | collective-permute-done | bytes 544 | tf_op jit(solution)/shard_map/ppermute | solution.py:21
  154.6 2.0 collective-permute-start.21
  156.6 2.6 %collective-permute-start.22 = (f32[1,1,1,128]{3,2,1,0:T(1,128)S(1)}, f32[1,1,1,128]{3,2,1,0:T(1,128)S(1)}, u32[]{:S(2)}, u32[]{:S(2)}) collective-permute-start(f32[1,1,1,128]{3,2,1,0:T(1,128)S(1)} %fusion.150), channel_id=1, source_target_pairs={{1,0},{2,1},{3,2},{4,3},{5,4},{6,5},{7,6},{8,7},{9,8},{10,9},{11,1... | collective-permute-start | bytes 1544 | tf_op jit(solution)/shard_map/ppermute | solution.py:21
  159.1 4.1 %collective-permute-done.22 = f32[1,1,1,128]{3,2,1,0:T(1,128)S(1)} collective-permute-done((f32[1,1,1,128]{3,2,1,0:T(1,128)S(1)}, f32[1,1,1,128]{3,2,1,0:T(1,128)S(1)}, u32[]{:S(2)}, u32[]{:S(2)}) %collective-permute-start.22) | collective-permute-done | bytes 544 | tf_op jit(solution)/shard_map/ppermute | solution.py:21
  171.6 2.0 collective-permute-start.23
  173.6 2.3 collective-permute-start.24
  176.0 4.3 %collective-permute-done.24 = f32[2,2,2,128]{3,2,1,0:T(2,128)S(1)} collective-permute-done((f32[2,2,2,128]{3,2,1,0:T(2,128)S(1)}, f32[2,2,2,128]{3,2,1,0:T(2,128)S(1)}, u32[]{:S(2)}, u32[]{:S(2)}) %collective-permute-start.24) | collective-permute-done | bytes 4128 | tf_op jit(solution)/shard_map/ppermute | solution.py:21
  186.8 1.9 collective-permute-start.25
  188.8 2.4 %collective-permute-start.26 = (f32[2,2,2,128]{3,2,1,0:T(2,128)S(1)}, f32[2,2,2,128]{3,2,1,0:T(2,128)S(1)}, u32[]{:S(2)}, u32[]{:S(2)}) collective-permute-start(f32[2,2,2,128]{3,2,1,0:T(2,128)S(1)} %add_select_fusion.5), channel_id=1, source_target_pairs={{1,0},{2,1},{3,2},{4,3},{5,4},{6,5},{7,6},{8,7},{9,8},{10,9},{11,1... | collective-permute-start | bytes 12296 | tf_op jit(solution)/shard_map/ppermute | solution.py:21
  191.2 4.3 %collective-permute-done.26 = f32[2,2,2,128]{3,2,1,0:T(2,128)S(1)} collective-permute-done((f32[2,2,2,128]{3,2,1,0:T(2,128)S(1)}, f32[2,2,2,128]{3,2,1,0:T(2,128)S(1)}, u32[]{:S(2)}, u32[]{:S(2)}) %collective-permute-start.26) | collective-permute-done | bytes 4128 | tf_op jit(solution)/shard_map/ppermute | solution.py:21
  202.2 1.9 collective-permute-start.27
  204.1 2.4 %collective-permute-start.28 = (f32[4,4,4,128]{3,2,1,0:T(4,128)S(1)}, f32[4,4,4,128]{3,2,1,0:T(4,128)S(1)}, u32[]{:S(2)}, u32[]{:S(2)}) collective-permute-start(f32[4,4,4,128]{3,2,1,0:T(4,128)S(1)} %select_add_fusion), channel_id=1, source_target_pairs={{1,0},{2,1},{3,2},{4,3},{5,4},{6,5},{7,6},{8,7},{9,8},{10,9},{11,1... | collective-permute-start | bytes 98312 | tf_op jit(solution)/shard_map/ppermute | solution.py:21
  206.6 4.6 %collective-permute-done.28 = f32[4,4,4,128]{3,2,1,0:T(4,128)S(1)} collective-permute-done((f32[4,4,4,128]{3,2,1,0:T(4,128)S(1)}, f32[4,4,4,128]{3,2,1,0:T(4,128)S(1)}, u32[]{:S(2)}, u32[]{:S(2)}) %collective-permute-start.28) | collective-permute-done | bytes 32800 | tf_op jit(solution)/shard_map/ppermute | solution.py:21
  218.8 1.9 collective-permute-start.29
  220.7 2.7 %collective-permute-start.30 = (f32[4,4,4,128]{3,2,1,0:T(4,128)S(1)}, f32[4,4,4,128]{3,2,1,0:T(4,128)S(1)}, u32[]{:S(2)}, u32[]{:S(2)}) collective-permute-start(f32[4,4,4,128]{3,2,1,0:T(4,128)S(1)} %add_select_fusion.1), channel_id=1, source_target_pairs={{1,0},{2,1},{3,2},{4,3},{5,4},{6,5},{7,6},{8,7},{9,8},{10,9},{11,1... | collective-permute-start | bytes 98312 | tf_op jit(solution)/shard_map/ppermute | solution.py:21
  223.4 4.3 %collective-permute-done.30 = f32[4,4,4,128]{3,2,1,0:T(4,128)S(1)} collective-permute-done((f32[4,4,4,128]{3,2,1,0:T(4,128)S(1)}, f32[4,4,4,128]{3,2,1,0:T(4,128)S(1)}, u32[]{:S(2)}, u32[]{:S(2)}) %collective-permute-start.30) | collective-permute-done | bytes 32800 | tf_op jit(solution)/shard_map/ppermute | solution.py:21
  (372 shorter events, 99.3 us)
Async XLA Ops:
  0.0 0.7 copy-start.4
  2.7 6.4 %collective-permute-start = (f32[4,4,4,128]{3,2,1,0:T(4,128)S(1)}, f32[4,4,4,128]{3,2,1,0:T(4,128)S(1)}, u32[]{:S(2)}, u32[]{:S(2)}) collective-permute-start(f32[4,4,4,128]{3,2,1,0:T(4,128)S(1)} %broadcast_select_fusion.1), channel_id=1, source_target_pairs={{0,1},{1,2},{2,3},{3,4},{4,5},{5,6},{6,7},{7,8},{8,9},{9,10},{10,1... | collective-permute-start | bytes 98312 | tf_op jit(solution)/shard_map/ppermute | solution.py:20
  6.3 7.0 %collective-permute-start.1 = (f32[4,4,4,128]{3,2,1,0:T(4,128)S(1)}, f32[4,4,4,128]{3,2,1,0:T(4,128)S(1)}, u32[]{:S(2)}, u32[]{:S(2)}) collective-permute-start(f32[4,4,4,128]{3,2,1,0:T(4,128)S(1)} %broadcast_select_fusion.1), channel_id=1, source_target_pairs={{1,0},{2,1},{3,2},{4,3},{5,4},{6,5},{7,6},{8,7},{9,8},{10,9},{11,1... | collective-permute-start | bytes 98312 | tf_op jit(solution)/shard_map/ppermute | solution.py:21
  8.3 0.7 copy-start.3
  20.8 0.8 copy-start.2
  20.9 0.8 copy-start.1
  20.9 0.8 copy-start
  21.7 4.4 %collective-permute-start.2 = (f32[4,4,4,128]{3,2,1,0:T(4,128)S(1)}, f32[4,4,4,128]{3,2,1,0:T(4,128)S(1)}, u32[]{:S(2)}, u32[]{:S(2)}) collective-permute-start(f32[4,4,4,128]{3,2,1,0:T(4,128)S(1)} %add_select_fusion.3), channel_id=1, source_target_pairs={{0,1},{1,2},{2,3},{3,4},{4,5},{5,6},{6,7},{7,8},{8,9},{9,10},{10,1... | collective-permute-start | bytes 98312 | tf_op jit(solution)/shard_map/ppermute | solution.py:20
  23.7 7.0 %collective-permute-start.3 = (f32[4,4,4,128]{3,2,1,0:T(4,128)S(1)}, f32[4,4,4,128]{3,2,1,0:T(4,128)S(1)}, u32[]{:S(2)}, u32[]{:S(2)}) collective-permute-start(f32[4,4,4,128]{3,2,1,0:T(4,128)S(1)} %add_select_fusion.3), channel_id=1, source_target_pairs={{1,0},{2,1},{3,2},{4,3},{5,4},{6,5},{7,6},{8,7},{9,8},{10,9},{11,1... | collective-permute-start | bytes 98312 | tf_op jit(solution)/shard_map/ppermute | solution.py:21
  38.3 4.4 %collective-permute-start.4 = (f32[4,4,4,128]{3,2,1,0:T(4,128)S(1)}, f32[4,4,4,128]{3,2,1,0:T(4,128)S(1)}, u32[]{:S(2)}, u32[]{:S(2)}) collective-permute-start(f32[4,4,4,128]{3,2,1,0:T(4,128)S(1)} %add_select_fusion.2), channel_id=1, source_target_pairs={{0,1},{1,2},{2,3},{3,4},{4,5},{5,6},{6,7},{7,8},{8,9},{9,10},{10,1... | collective-permute-start | bytes 98312 | tf_op jit(solution)/shard_map/ppermute | solution.py:20
  40.3 7.0 %collective-permute-start.5 = (f32[4,4,4,128]{3,2,1,0:T(4,128)S(1)}, f32[4,4,4,128]{3,2,1,0:T(4,128)S(1)}, u32[]{:S(2)}, u32[]{:S(2)}) collective-permute-start(f32[4,4,4,128]{3,2,1,0:T(4,128)S(1)} %add_select_fusion.2), channel_id=1, source_target_pairs={{1,0},{2,1},{3,2},{4,3},{5,4},{6,5},{7,6},{8,7},{9,8},{10,9},{11,1... | collective-permute-start | bytes 98312 | tf_op jit(solution)/shard_map/ppermute | solution.py:21
  55.0 4.6 %collective-permute-start.6 = (f32[2,2,2,128]{3,2,1,0:T(2,128)S(1)}, f32[2,2,2,128]{3,2,1,0:T(2,128)S(1)}, u32[]{:S(2)}, u32[]{:S(2)}) collective-permute-start(f32[2,2,2,128]{3,2,1,0:T(2,128)S(1)} %fusion.89), channel_id=1, source_target_pairs={{0,1},{1,2},{2,3},{3,4},{4,5},{5,6},{6,7},{7,8},{8,9},{9,10},{10,1... | collective-permute-start | bytes 12296 | tf_op jit(solution)/shard_map/ppermute | solution.py:20
  56.9 6.7 %collective-permute-start.7 = (f32[2,2,2,128]{3,2,1,0:T(2,128)S(1)}, f32[2,2,2,128]{3,2,1,0:T(2,128)S(1)}, u32[]{:S(2)}, u32[]{:S(2)}) collective-permute-start(f32[2,2,2,128]{3,2,1,0:T(2,128)S(1)} %fusion.89), channel_id=1, source_target_pairs={{1,0},{2,1},{3,2},{4,3},{5,4},{6,5},{7,6},{8,7},{9,8},{10,9},{11,1... | collective-permute-start | bytes 12296 | tf_op jit(solution)/shard_map/ppermute | solution.py:21
  70.2 4.4 %collective-permute-start.8 = (f32[2,2,2,128]{3,2,1,0:T(2,128)S(1)}, f32[2,2,2,128]{3,2,1,0:T(2,128)S(1)}, u32[]{:S(2)}, u32[]{:S(2)}) collective-permute-start(f32[2,2,2,128]{3,2,1,0:T(2,128)S(1)} %add_select_fusion.6), channel_id=1, source_target_pairs={{0,1},{1,2},{2,3},{3,4},{4,5},{5,6},{6,7},{7,8},{8,9},{9,10},{10,1... | collective-permute-start | bytes 12296 | tf_op jit(solution)/shard_map/ppermute | solution.py:20
  72.2 6.7 %collective-permute-start.9 = (f32[2,2,2,128]{3,2,1,0:T(2,128)S(1)}, f32[2,2,2,128]{3,2,1,0:T(2,128)S(1)}, u32[]{:S(2)}, u32[]{:S(2)}) collective-permute-start(f32[2,2,2,128]{3,2,1,0:T(2,128)S(1)} %add_select_fusion.6), channel_id=1, source_target_pairs={{1,0},{2,1},{3,2},{4,3},{5,4},{6,5},{7,6},{8,7},{9,8},{10,9},{11,1... | collective-permute-start | bytes 12296 | tf_op jit(solution)/shard_map/ppermute | solution.py:21
  86.1 4.3 %collective-permute-start.10 = (f32[1,1,1,128]{3,2,1,0:T(1,128)S(1)}, f32[1,1,1,128]{3,2,1,0:T(1,128)S(1)}, u32[]{:S(2)}, u32[]{:S(2)}) collective-permute-start(f32[1,1,1,128]{3,2,1,0:T(1,128)S(1)} %fusion.146), channel_id=1, source_target_pairs={{0,1},{1,2},{2,3},{3,4},{4,5},{5,6},{6,7},{7,8},{8,9},{9,10},{10,1... | collective-permute-start | bytes 1544 | tf_op jit(solution)/shard_map/ppermute | solution.py:20
  88.1 6.7 %collective-permute-start.11 = (f32[1,1,1,128]{3,2,1,0:T(1,128)S(1)}, f32[1,1,1,128]{3,2,1,0:T(1,128)S(1)}, u32[]{:S(2)}, u32[]{:S(2)}) collective-permute-start(f32[1,1,1,128]{3,2,1,0:T(1,128)S(1)} %fusion.146), channel_id=1, source_target_pairs={{1,0},{2,1},{3,2},{4,3},{5,4},{6,5},{7,6},{8,7},{9,8},{10,9},{11,1... | collective-permute-start | bytes 1544 | tf_op jit(solution)/shard_map/ppermute | solution.py:21
  103.1 4.3 %collective-permute-start.12 = (f32[1,1,1,128]{3,2,1,0:T(1,128)S(1)}, f32[1,1,1,128]{3,2,1,0:T(1,128)S(1)}, u32[]{:S(2)}, u32[]{:S(2)}) collective-permute-start(f32[1,1,1,128]{3,2,1,0:T(1,128)S(1)} %fusion.151), channel_id=1, source_target_pairs={{0,1},{1,2},{2,3},{3,4},{4,5},{5,6},{6,7},{7,8},{8,9},{9,10},{10,1... | collective-permute-start | bytes 1544 | tf_op jit(solution)/shard_map/ppermute | solution.py:20
  105.1 6.7 %collective-permute-start.13 = (f32[1,1,1,128]{3,2,1,0:T(1,128)S(1)}, f32[1,1,1,128]{3,2,1,0:T(1,128)S(1)}, u32[]{:S(2)}, u32[]{:S(2)}) collective-permute-start(f32[1,1,1,128]{3,2,1,0:T(1,128)S(1)} %fusion.151), channel_id=1, source_target_pairs={{1,0},{2,1},{3,2},{4,3},{5,4},{6,5},{7,6},{8,7},{9,8},{10,9},{11,1... | collective-permute-start | bytes 1544 | tf_op jit(solution)/shard_map/ppermute | solution.py:21
  120.3 1.2 collective-permute-start.14
  121.5 2.4 %collective-permute-start.15 = (f32[16]{0:T(128)S(1)}, f32[16]{0:T(128)S(1)}, u32[]{:S(2)}, u32[]{:S(2)}) collective-permute-start(f32[16]{0:T(128)S(1)} %fusion.152), channel_id=1, source_target_pairs={{0,2},{1,3},{2,0},{3,1},{4,6},{5,7},{6,4},{7,5},{8,10},{9,11},{10,... | collective-permute-start | bytes 200 | tf_op jit(solution)/shard_map/ppermute | solution.py:29
  123.9 2.4 %collective-permute-start.16 = (f32[16]{0:T(128)S(1)}, f32[16]{0:T(128)S(1)}, u32[]{:S(2)}, u32[]{:S(2)}) collective-permute-start(f32[16]{0:T(128)S(1)} %add.431), channel_id=1, source_target_pairs={{0,4},{1,5},{2,6},{3,7},{4,0},{5,1},{6,2},{7,3},{8,12},{9,13},{10,... | collective-permute-start | bytes 200 | tf_op jit(solution)/shard_map/ppermute | solution.py:29
  126.3 2.4 %collective-permute-start.17 = (f32[16]{0:T(128)S(1)}, f32[16]{0:T(128)S(1)}, u32[]{:S(2)}, u32[]{:S(2)}) collective-permute-start(f32[16]{0:T(128)S(1)} %add.433), channel_id=1, source_target_pairs={{0,8},{1,9},{2,10},{3,11},{4,12},{5,13},{6,14},{7,15},{8,0},{9,1},... | collective-permute-start | bytes 200 | tf_op jit(solution)/shard_map/ppermute | solution.py:29
  128.7 3.3 %collective-permute-start.18 = (f32[16]{0:T(128)S(1)}, f32[16]{0:T(128)S(1)}, u32[]{:S(2)}, u32[]{:S(2)}) collective-permute-start(f32[16]{0:T(128)S(1)} %add.435), channel_id=1, source_target_pairs={{0,16},{1,17},{2,18},{3,19},{4,20},{5,21},{6,22},{7,23},{8,24},{9,... | collective-permute-start | bytes 200 | tf_op jit(solution)/shard_map/ppermute | solution.py:29
  132.8 8.7 %collective-permute-start.19 = (f32[1,1,1,128]{3,2,1,0:T(1,128)S(1)}, f32[1,1,1,128]{3,2,1,0:T(1,128)S(1)}, u32[]{:S(2)}, u32[]{:S(2)}) collective-permute-start(f32[1,1,1,128]{3,2,1,0:T(1,128)S(1)} %select_add_fusion.2), channel_id=1, source_target_pairs={{0,1},{1,2},{2,3},{3,4},{4,5},{5,6},{6,7},{7,8},{8,9},{9,10},{10,1... | collective-permute-start | bytes 1544 | tf_op jit(solution)/shard_map/ppermute | solution.py:20
  139.6 6.7 %collective-permute-start.20 = (f32[1,1,1,128]{3,2,1,0:T(1,128)S(1)}, f32[1,1,1,128]{3,2,1,0:T(1,128)S(1)}, u32[]{:S(2)}, u32[]{:S(2)}) collective-permute-start(f32[1,1,1,128]{3,2,1,0:T(1,128)S(1)} %select_add_fusion.2), channel_id=1, source_target_pairs={{1,0},{2,1},{3,2},{4,3},{5,4},{6,5},{7,6},{8,7},{9,8},{10,9},{11,1... | collective-permute-start | bytes 1544 | tf_op jit(solution)/shard_map/ppermute | solution.py:21
  154.6 4.6 %collective-permute-start.21 = (f32[1,1,1,128]{3,2,1,0:T(1,128)S(1)}, f32[1,1,1,128]{3,2,1,0:T(1,128)S(1)}, u32[]{:S(2)}, u32[]{:S(2)}) collective-permute-start(f32[1,1,1,128]{3,2,1,0:T(1,128)S(1)} %fusion.150), channel_id=1, source_target_pairs={{0,1},{1,2},{2,3},{3,4},{4,5},{5,6},{6,7},{7,8},{8,9},{9,10},{10,1... | collective-permute-start | bytes 1544 | tf_op jit(solution)/shard_map/ppermute | solution.py:20
  156.6 6.7 %collective-permute-start.22 = (f32[1,1,1,128]{3,2,1,0:T(1,128)S(1)}, f32[1,1,1,128]{3,2,1,0:T(1,128)S(1)}, u32[]{:S(2)}, u32[]{:S(2)}) collective-permute-start(f32[1,1,1,128]{3,2,1,0:T(1,128)S(1)} %fusion.150), channel_id=1, source_target_pairs={{1,0},{2,1},{3,2},{4,3},{5,4},{6,5},{7,6},{8,7},{9,8},{10,9},{11,1... | collective-permute-start | bytes 1544 | tf_op jit(solution)/shard_map/ppermute | solution.py:21
  171.6 4.4 %collective-permute-start.23 = (f32[2,2,2,128]{3,2,1,0:T(2,128)S(1)}, f32[2,2,2,128]{3,2,1,0:T(2,128)S(1)}, u32[]{:S(2)}, u32[]{:S(2)}) collective-permute-start(f32[2,2,2,128]{3,2,1,0:T(2,128)S(1)} %select_add_fusion.1), channel_id=1, source_target_pairs={{0,1},{1,2},{2,3},{3,4},{4,5},{5,6},{6,7},{7,8},{8,9},{9,10},{10,1... | collective-permute-start | bytes 12296 | tf_op jit(solution)/shard_map/ppermute | solution.py:20
  173.6 6.7 %collective-permute-start.24 = (f32[2,2,2,128]{3,2,1,0:T(2,128)S(1)}, f32[2,2,2,128]{3,2,1,0:T(2,128)S(1)}, u32[]{:S(2)}, u32[]{:S(2)}) collective-permute-start(f32[2,2,2,128]{3,2,1,0:T(2,128)S(1)} %select_add_fusion.1), channel_id=1, source_target_pairs={{1,0},{2,1},{3,2},{4,3},{5,4},{6,5},{7,6},{8,7},{9,8},{10,9},{11,1... | collective-permute-start | bytes 12296 | tf_op jit(solution)/shard_map/ppermute | solution.py:21
  186.8 4.4 %collective-permute-start.25 = (f32[2,2,2,128]{3,2,1,0:T(2,128)S(1)}, f32[2,2,2,128]{3,2,1,0:T(2,128)S(1)}, u32[]{:S(2)}, u32[]{:S(2)}) collective-permute-start(f32[2,2,2,128]{3,2,1,0:T(2,128)S(1)} %add_select_fusion.5), channel_id=1, source_target_pairs={{0,1},{1,2},{2,3},{3,4},{4,5},{5,6},{6,7},{7,8},{8,9},{9,10},{10,1... | collective-permute-start | bytes 12296 | tf_op jit(solution)/shard_map/ppermute | solution.py:20
  188.8 6.7 %collective-permute-start.26 = (f32[2,2,2,128]{3,2,1,0:T(2,128)S(1)}, f32[2,2,2,128]{3,2,1,0:T(2,128)S(1)}, u32[]{:S(2)}, u32[]{:S(2)}) collective-permute-start(f32[2,2,2,128]{3,2,1,0:T(2,128)S(1)} %add_select_fusion.5), channel_id=1, source_target_pairs={{1,0},{2,1},{3,2},{4,3},{5,4},{6,5},{7,6},{8,7},{9,8},{10,9},{11,1... | collective-permute-start | bytes 12296 | tf_op jit(solution)/shard_map/ppermute | solution.py:21
  202.2 4.4 %collective-permute-start.27 = (f32[4,4,4,128]{3,2,1,0:T(4,128)S(1)}, f32[4,4,4,128]{3,2,1,0:T(4,128)S(1)}, u32[]{:S(2)}, u32[]{:S(2)}) collective-permute-start(f32[4,4,4,128]{3,2,1,0:T(4,128)S(1)} %select_add_fusion), channel_id=1, source_target_pairs={{0,1},{1,2},{2,3},{3,4},{4,5},{5,6},{6,7},{7,8},{8,9},{9,10},{10,1... | collective-permute-start | bytes 98312 | tf_op jit(solution)/shard_map/ppermute | solution.py:20
  204.1 7.0 %collective-permute-start.28 = (f32[4,4,4,128]{3,2,1,0:T(4,128)S(1)}, f32[4,4,4,128]{3,2,1,0:T(4,128)S(1)}, u32[]{:S(2)}, u32[]{:S(2)}) collective-permute-start(f32[4,4,4,128]{3,2,1,0:T(4,128)S(1)} %select_add_fusion), channel_id=1, source_target_pairs={{1,0},{2,1},{3,2},{4,3},{5,4},{6,5},{7,6},{8,7},{9,8},{10,9},{11,1... | collective-permute-start | bytes 98312 | tf_op jit(solution)/shard_map/ppermute | solution.py:21
  218.8 4.7 %collective-permute-start.29 = (f32[4,4,4,128]{3,2,1,0:T(4,128)S(1)}, f32[4,4,4,128]{3,2,1,0:T(4,128)S(1)}, u32[]{:S(2)}, u32[]{:S(2)}) collective-permute-start(f32[4,4,4,128]{3,2,1,0:T(4,128)S(1)} %add_select_fusion.1), channel_id=1, source_target_pairs={{0,1},{1,2},{2,3},{3,4},{4,5},{5,6},{6,7},{7,8},{8,9},{9,10},{10,1... | collective-permute-start | bytes 98312 | tf_op jit(solution)/shard_map/ppermute | solution.py:20
  220.7 7.0 %collective-permute-start.30 = (f32[4,4,4,128]{3,2,1,0:T(4,128)S(1)}, f32[4,4,4,128]{3,2,1,0:T(4,128)S(1)}, u32[]{:S(2)}, u32[]{:S(2)}) collective-permute-start(f32[4,4,4,128]{3,2,1,0:T(4,128)S(1)} %add_select_fusion.1), channel_id=1, source_target_pairs={{1,0},{2,1},{3,2},{4,3},{5,4},{6,5},{7,6},{8,7},{9,8},{10,9},{11,1... | collective-permute-start | bytes 98312 | tf_op jit(solution)/shard_map/ppermute | solution.py:21
where the time goes:
time: 237 us; the launch traced here: 236 us
  local copies, waits for them, and re-layouts  95.6 us (40%)
  waiting for transfers between devices  67 us (28%)
  starting transfers between devices  63.8 us (27%)
  other arithmetic  7.63 us (3%)
    gather x132, local copies, waits for them, and re-layouts, neighbour_total(): face = jnp.take(face, safe, axis=3) * valid  75.7 us
    ppermute x13, waiting for transfers between devices, padded(): after = lax.ppermute(leading, axis, down)  56.6 us
    ppermute x13, starting transfers between devices, padded(): before = lax.ppermute(last, axis, up)  31.9 us
    ppermute x13, starting transfers between devices, padded(): after = lax.ppermute(leading, axis, down)  30.7 us
    unnamed x46, local copies, waits for them, and re-layouts  13.1 us
    ppermute x5, waiting for transfers between devices, partner(): return lax.ppermute(value, axis, pairs)  10.4 us
    another operation x18, local copies, waits for them, and re-layouts, neighbour_total(): face = jnp.take(face, safe, axis=3) * valid  5.36 us
  transfers between devices with their start and end apart: 31, of which 18 were waited for; matrix products, arithmetic and copies ran while one was open for 0% of the time, Pallas kernels for 0%

commit v1 on v0

v1 whole, which is shorter than its diff:
```python
import jax
import jax.numpy as jnp
from jax import lax
from jax.experimental import pallas as pl
from jax.experimental.pallas import tpu as pltpu
from jax.sharding import PartitionSpec as P

OMEGA = 0.8
COARSE = 8.0
EXCHANGES = 13
RIM = 8
STAGE_BITS = 5
MESH = pl.DeviceIdType.MESH


def lanes_of(values, index):
    return jnp.take_along_axis(values, index, axis=1, mode="promise_in_bounds")


def rows_of(values, index):
    return jnp.take_along_axis(values, index, axis=0, mode="promise_in_bounds")


def stages_of(devices):
    bits, low, stages = devices.bit_length() - 1, 0, []
    while low < bits:
        take = min(STAGE_BITS, bits - low)
        stages.append((low, take))
        low += take
    return stages


def cycle_kernel(
    devices, slots, counts, rhs, screen, guess, neighbours, out,
    pack, halo, sums, own, halo_send, halo_recv, sum_send, sum_recv,
):
    rank = lax.axis_index("sfc")
    before = lax.rem(rank + devices - 1, devices)
    after = lax.rem(rank + 1, devices)
    stages = stages_of(devices)

    def member(stage, place):
        low, bits = stage
        mine = lax.rem(rank // 2**low, 2**bits)
        return rank + (lax.rem(mine + place, 2**bits) - mine) * 2**low

    barrier = pltpu.get_barrier_semaphore()
    greeted = 0
    for target in (before, after):
        pl.semaphore_signal(barrier, inc=1, device_id=(target,), device_id_type=MESH)
        greeted += 1
    for stage in stages:
        for place in range(1, 2 ** stage[1]):
            pl.semaphore_signal(barrier, inc=1, device_id=(member(stage, place),), device_id_type=MESH)
            greeted += 1

    tile = (8, slots)
    sub = lax.broadcasted_iota(jnp.int32, tile, 0)
    lane = lax.broadcasted_iota(jnp.int32, tile, 1)
    live_own = counts[rank]
    live_before = counts[before]
    live = lane < live_own
    bits = [(sub & (4 >> a)) != 0 for a in range(3)]
    flips = [sub ^ (4 >> a) for a in range(3)]
    half = slots // 2

    pack_index = (lane & (RIM - 1)) + jnp.where(lane < half, live_own - RIM, 0)
    pack_place = (lane & (half - 1)) // RIM

    def decode(code):
        inside = (code >= slots) & (code < 2 * slots)
        outside = (code >= 0) & jnp.logical_not(inside)
        local = jnp.where(inside, code - slots, 0)
        off = jnp.where(code < slots, code - (live_before - RIM), half + code - 2 * slots)
        return inside, outside, local, jnp.where(outside, off & (slots - 1), 0)

    codes = [jnp.broadcast_to(neighbours[k : k + 1, :], tile) for k in range(6)]
    sided = [decode(jnp.where(bits[a], codes[2 * a], codes[2 * a + 1])) for a in range(3)]
    taker = [decode(jnp.where(bits[a], codes[2 * a + 1], codes[2 * a])) for a in range(3)]
    every = jnp.full(tile, -1, jnp.int32)
    for k in range(6):
        every = jnp.where(sub == k, codes[k], every)
    every = decode(every)

    first, second = (sub & 1) + ((sub >> 1) & 1) * 4, (sub & 1) + ((sub >> 1) & 1) * 4 + 2

    def load(ref):
        rows = [ref[8 * t : 8 * t + 8, :] for t in range(8)]
        result = []
        for hx in range(2):
            for hy in range(2):
                low, high = rows[4 * hx + hy], rows[4 * hx + 2 + hy]
                for index in (first, second):
                    result.append(jnp.where(sub < 4, rows_of(low, index), rows_of(high, index)))
        return result

    copies = []
    state = {"step": 0, "ready": False}

    def begin(packed):
        step = state["step"]
        state["step"] = step + 1
        pack[step] = packed
        if not state["ready"]:
            pl.semaphore_wait(barrier, greeted)
            state["ready"] = True
        pair = []
        for side, target in ((0, after), (1, before)):
            copy = pltpu.make_async_remote_copy(
                src_ref=pack.at[step],
                dst_ref=halo.at[step, side],
                send_sem=halo_send.at[step, side],
                recv_sem=halo_recv.at[step, side],
                device_id=(target,),
                device_id_type=MESH,
            )
            copy.start()
            pair.append(copy)
        copies.extend(pair)
        return step, pair

    def finish(handle):
        step, pair = handle
        for copy in pair:
            copy.wait_recv()
        return jnp.where(lane < half, halo[step, 0], halo[step, 1])

    def total_fine(values):
        packed = jnp.zeros(tile, jnp.float32)
        for j in range(8):
            packed = jnp.where(pack_place == j, lanes_of(values[j], pack_index), packed)
        handle = begin(packed)
        sums_here = [None] * 8
        for a in range(3):
            stride = 4 >> a
            inside, _, local, _ = sided[a]
            for j in range(8):
                if j & stride:
                    continue
                low, high = values[j], values[j + stride]
                across = jnp.where(inside, lanes_of(jnp.where(bits[a], high, low), local), 0.0)
                for place, part in (
                    (j, low + jnp.where(bits[a], across, high)),
                    (j + stride, high + jnp.where(bits[a], low, across)),
                ):
                    part = rows_of(part, flips[a])
                    sums_here[place] = part if sums_here[place] is None else sums_here[place] + part
        received = finish(handle)
        for a in range(3):
            stride = 4 >> a
            _, outside, _, off = taker[a]
            turned = rows_of(received, flips[a])
            base = off + jnp.where(bits[a], 0, RIM * stride)
            for j in range(8):
                if j & stride:
                    continue
                got = jnp.where(outside, lanes_of(turned, (base + RIM * j) & (slots - 1)), 0.0)
                sums_here[j] = sums_here[j] + jnp.where(bits[a], 0.0, got)
                sums_here[j + stride] = sums_here[j + stride] + jnp.where(bits[a], got, 0.0)
        return sums_here

    def total_middle(values):
        values = values[0]
        handle = begin(lanes_of(values, pack_index))
        total = jnp.zeros(tile, jnp.float32)
        for a in range(3):
            inside, _, local, _ = sided[a]
            total = total + rows_of(values + jnp.where(inside, lanes_of(values, local), 0.0), flips[a])
        received = finish(handle)
        for a in range(3):
            _, outside, _, off = taker[a]
            total = total + jnp.where(outside, lanes_of(rows_of(received, flips[a]), off), 0.0)
        return [total]

    def total_coarse(values):
        values = values[0]
        handle = begin(lanes_of(values, pack_index))
        inside, outside, local, off = every
        part = jnp.where(inside, lanes_of(values, local), 0.0)
        part = part + jnp.where(outside, lanes_of(finish(handle), off), 0.0)
        return [jnp.broadcast_to(part.sum(axis=0, keepdims=True), tile)]

    totals = (total_fine, total_middle, total_coarse)

    def masked(values):
        return [jnp.where(live, v, 0.0) for v in values]

    def sweep(depth, values, forcing, weight):
        found = totals[depth](values)
        return [(1.0 - OMEGA) * v + w * (f + t) for v, f, w, t in zip(values, forcing, weight, found)]

    def defect_of(depth, values, forcing, diagonal):
        found = totals[depth](values)
        return [jnp.where(live, f - (d * v - t), 0.0) for v, f, d, t in zip(values, forcing, diagonal, found)]

    def stacked(rows):
        result = jnp.broadcast_to(rows[0], tile)
        for j in range(1, 8):
            result = jnp.where(sub == j, rows[j], result)
        return result

    def restrict(depth, values):
        if depth == 0:
            return [stacked([v.sum(axis=0, keepdims=True) * 0.5 for v in values])]
        return [jnp.broadcast_to(values[0].sum(axis=0, keepdims=True) * 0.5, tile)]

    def prolong(depth, values):
        if depth == 0:
            return [jnp.broadcast_to(values[0][j : j + 1, :], tile) for j in range(8)]
        return values

    forcing = masked(load(rhs))
    screening = masked(load(screen))
    current = masked(load(guess))
    levels = []
    for depth in range(3):
        diagonal = [6.0 + s for s in screening]
        weight = masked([OMEGA / d for d in diagonal])
        if depth == 0:
            current = sweep(depth, current, forcing, weight)
        else:
            current = [w * f for w, f in zip(weight, forcing)]
        current = sweep(depth, current, forcing, weight)
        levels.append((current, forcing, weight))
        defect = defect_of(depth, current, forcing, diagonal)
        if depth < 2:
            forcing, screening = restrict(depth, defect), restrict(depth, screening)

    grouped = defect[0]
    for distance in (1, 2, 4):
        grouped = grouped + lanes_of(grouped, lane ^ distance)
    running = grouped[0:1, :] * 0.5
    correction = running / COARSE
    start = 0
    for number, stage in enumerate(stages):
        low, count = stage
        size = 2**count
        own[number] = running
        group = []
        for place in range(1, size):
            copy = pltpu.make_async_remote_copy(
                src_ref=own.at[number],
                dst_ref=sums.at[start + place],
                send_sem=sum_send.at[start + place],
                recv_sem=sum_recv.at[start + place],
                device_id=(member(stage, place),),
                device_id_type=MESH,
            )
            copy.start()
            group.append(copy)
        copies.extend(group)
        mine = lax.rem(rank // 2**low, size)
        own_weight = sum(1.0 / (COARSE * 2 ** (low + k)) for k in range(1, count + 1))
        correction = correction + own_weight * running
        for place, copy in enumerate(group, 1):
            copy.wait_recv()
            sender = lax.rem(mine - place + size, size)
            factor = jnp.float32(0.0)
            for k in range(1, count + 1):
                same = (mine // 2**k) == (sender // 2**k)
                factor = factor + jnp.where(same, 1.0 / (COARSE * 2 ** (low + k)), 0.0)
            arrived = sums[start + place]
            correction = correction + factor * arrived
            running = running + arrived
        start += size

    current = [jnp.broadcast_to(correction, tile)]
    for depth in (2, 1, 0):
        kept, forcing, weight = levels[depth]
        raised = current if depth == 2 else prolong(depth, current)
        current = [a + b for a, b in zip(kept, masked(raised))]
        for _ in range(2):
            current = sweep(depth, current, forcing, weight)

    spread = (sub & 1) + (sub >> 2) * 2
    upper = (sub & 2) != 0
    for hx in range(2):
        for hy in range(2):
            near, far = current[4 * hx + 2 * hy], current[4 * hx + 2 * hy + 1]
            for bx in range(2):
                row = 8 * (4 * hx + 2 * bx + hy)
                index = spread + 4 * bx
                out[row : row + 8, :] = jnp.where(upper, rows_of(far, index), rows_of(near, index))
    for copy in copies:
        copy.wait_send()


def per_device(rhs, screen, guess, counts, neighbours):
    shape = rhs.shape
    slots = shape[3]
    devices = lax.axis_size("sfc")
    stages = stages_of(devices)
    places = max(1, sum(2**count for _, count in stages))
    rows = shape[0] * shape[1] * shape[2]
    vmem = pl.BlockSpec(memory_space=pltpu.VMEM)
    result = pl.pallas_call(
        lambda *refs: cycle_kernel(devices, slots, *refs),
        out_shape=jax.ShapeDtypeStruct((rows, slots), jnp.float32),
        in_specs=[pl.BlockSpec(memory_space=pltpu.SMEM)] + [vmem] * 4,
        out_specs=vmem,
        scratch_shapes=[
            pltpu.VMEM((EXCHANGES, 8, slots), jnp.float32),
            pltpu.VMEM((EXCHANGES, 2, 8, slots), jnp.float32),
            pltpu.VMEM((places, 1, slots), jnp.float32),
            pltpu.VMEM((max(1, len(stages)), 1, slots), jnp.float32),
            pltpu.SemaphoreType.DMA((EXCHANGES, 2)),
            pltpu.SemaphoreType.DMA((EXCHANGES, 2)),
            pltpu.SemaphoreType.DMA((places,)),
            pltpu.SemaphoreType.DMA((places,)),
        ],
        compiler_params=pltpu.CompilerParams(collective_id=0, has_side_effects=True),
        name="cycle",
    )(counts, rhs.reshape(rows, slots), screen.reshape(rows, slots), guess.reshape(rows, slots), neighbours)
    return result.reshape(shape)


def solution(mesh):
    blocks = P(None, None, None, "sfc")
    return jax.shard_map(
        per_device,
        mesh=mesh,
        in_specs=(blocks, blocks, blocks, P(), P(None, "sfc")),
        out_specs=blocks,
        check_vma=False,
    )
```

time: 237 us -> 69.6 us (0.29)
  the two profiles are of different devices: /device:TPU:15 before, /device:TPU:0 now
where the time goes in v1:
time: 69.6 us; the launch traced here: 69.4 us
  Pallas kernels  68 us (98%)
  local copies, waits for them, and re-layouts  1.38 us (2%)
    pallas_call x1, Pallas kernels, per_device(): pl.pallas_call(lambda *refs: cycle_kernel(devices, slots, *refs), out_sha...  68 us

profile of v1, /device:TPU:0, one launch (start us, length us, event | category | flops | bytes accessed | tf_op | source)
XLA Modules:
  0.0 69.4 jit_solution(15874995302577386614)
XLA Ops:
  0.0 68.0 %cycle.1 = f32[64,128]{1,0:T(8,128)} custom-call(s32[32]{0:T(128)} %refs_0_.1, f32[64,128]{1,0:T(8,128)} %bitcast.5, f32[64,128]{1,0:T(8,128)} %bitcast.6, f32[64,128]{1,0:T(8,128)} %bitcast.7, s32[6,128]{1,0:T(8,128)} %refs_4_.1), custom_call_target="tpu_custom_call" | custom-call | tf_op jit(solution)/shard_map/cycle/pallas_call | solution.py:296
  68.0 1.4 %copy.7 = f32[4,4,4,128]{3,2,1,0:T(4,128)} copy(f32[4,4,4,128]{3,2,1,0:T(4,128)} %bitcast.4) | data formatting | bytes 65536

commit v2 on v0

v2 whole, which is shorter than its diff:
```python
import jax
import jax.numpy as jnp
from jax import lax
from jax.experimental import pallas as pl
from jax.experimental.pallas import tpu as pltpu
from jax.sharding import PartitionSpec as P

OMEGA = 0.8
COARSE = 8.0
RIM = 8
REACH = 3
MESH = pl.DeviceIdType.MESH


def lanes_of(values, index):
    return jnp.take_along_axis(values, index, axis=1, mode="promise_in_bounds")


def rows_of(values, index):
    return jnp.take_along_axis(values, index, axis=0, mode="promise_in_bounds")


def cycle_kernel(
    devices, slots, counts, rhs, screen, guess, neighbours, out,
    near, rim, codes, middle, fine, coarse, sums, tree,
    rim_out, middle_out, fine_out, coarse_out, send_sem, recv_sem,
):
    rank = lax.axis_index("sfc")

    def at(offset):
        return lax.rem(rank + offset + devices, devices)

    barrier = pltpu.get_barrier_semaphore()
    for offset in range(1, devices):
        pl.semaphore_signal(barrier, inc=1, device_id=(at(offset),), device_id_type=MESH)

    tile = (8, slots)
    sub = lax.broadcasted_iota(jnp.int32, tile, 0)
    lane = lax.broadcasted_iota(jnp.int32, tile, 1)
    bits = [(sub & (4 >> a)) != 0 for a in range(3)]
    flips = [sub ^ (4 >> a) for a in range(3)]
    half = slots // 2
    live_of = {j: counts[at(j)] for j in range(-REACH - 1, REACH + 1)}
    live = {j: lane < live_of[j] for j in range(-REACH, REACH + 1)}

    pack_place = (lane & (half - 1)) // RIM
    pack_index = {
        j: (lane & (RIM - 1)) + jnp.where(lane < half, live_of[j] - RIM, 0)
        for j in range(-REACH, REACH + 1)
    }

    copies = []

    def send(source, target, offset):
        number = len(copies)
        copy = pltpu.make_async_remote_copy(
            src_ref=source,
            dst_ref=target,
            send_sem=send_sem.at[number],
            recv_sem=recv_sem.at[number],
            device_id=(at(offset),),
            device_id_type=MESH,
        )
        copy.start()
        copies.append(copy)
        return copy

    def place(offset, reach):
        return offset + reach if offset < 0 else offset + reach - 1

    def offsets(reach):
        return [sign * step for step in range(1, reach + 1) for sign in (1, -1)]

    first = (sub & 1) + ((sub >> 1) & 1) * 4

    def load(ref, *lead):
        rows = [ref[(*lead, slice(8 * t, 8 * t + 8), slice(None))] for t in range(8)]
        result = []
        for hx in range(2):
            for hy in range(2):
                low, high = rows[4 * hx + hy], rows[4 * hx + 2 + hy]
                for index in (first, first + 2):
                    result.append(jnp.where(sub < 4, rows_of(low, index), rows_of(high, index)))
        return result

    def masked(part, values):
        return [jnp.where(live[part], v, 0.0) for v in values]

    def packed(part, values):
        if len(values) == 1:
            return lanes_of(values[0], pack_index[part])
        result = lanes_of(values[0], pack_index[part])
        for j in range(1, 8):
            result = jnp.where(pack_place == j, lanes_of(values[j], pack_index[part]), result)
        return result

    forcing, screening, current = ({0: masked(0, load(r))} for r in (rhs, screen, guess))
    rim_out[...] = packed(0, current[0])
    pl.semaphore_wait(barrier, devices - 1)
    arrive = {}
    for o in offsets(2)[2:]:
        arrive["rim", -o] = send(rim_out, rim.at[place(-o, 2) // 3], o)
    for o in offsets(1):
        for k, ref in enumerate((guess, rhs, screen)):
            arrive["near", -o, k] = send(ref, near.at[place(-o, 1), k], o)
    for o in offsets(REACH):
        arrive["codes", -o] = send(neighbours, codes.at[place(-o, REACH)], o)

    def decoded(part, code):
        inside = (code >= slots) & (code < 2 * slots)
        outside = (code >= 0) & jnp.logical_not(inside)
        local = jnp.where(inside, code - slots, 0)
        off = jnp.where(code < slots, code - (live_of[part - 1] - RIM), half + code - 2 * slots)
        return inside, outside, local, jnp.where(outside, off & (slots - 1), 0)

    tables = {}

    def table(part):
        if part not in tables:
            if part:
                arrive["codes", part].wait_recv()
                ref = codes.at[place(part, REACH)]
            else:
                ref = neighbours
            rows = [jnp.broadcast_to(ref[k : k + 1, :], tile) for k in range(6)]
            sided = [decoded(part, jnp.where(bits[a], rows[2 * a], rows[2 * a + 1])) for a in range(3)]
            taker = [decoded(part, jnp.where(bits[a], rows[2 * a + 1], rows[2 * a])) for a in range(3)]
            every = jnp.full(tile, -1, jnp.int32)
            for k in range(6):
                every = jnp.where(sub == k, rows[k], every)
            tables[part] = (sided, taker, decoded(part, every))
        return tables[part]

    def total_fine(part, values, received):
        sided, taker, _ = table(part)
        total = [None] * 8
        for a in range(3):
            stride = 4 >> a
            inside, _, local, _ = sided[a]
            _, outside, _, off = taker[a]
            turned = rows_of(received, flips[a])
            base = off + jnp.where(bits[a], 0, RIM * stride)
            for j in range(8):
                if j & stride:
                    continue
                low, high = values[j], values[j + stride]
                across = jnp.where(inside, lanes_of(jnp.where(bits[a], high, low), local), 0.0)
                got = jnp.where(outside, lanes_of(turned, (base + RIM * j) & (slots - 1)), 0.0)
                for where, kept, far in (
                    (j, low + jnp.where(bits[a], across, high), jnp.where(bits[a], 0.0, got)),
                    (j + stride, high + jnp.where(bits[a], low, across), jnp.where(bits[a], got, 0.0)),
                ):
                    piece = rows_of(kept, flips[a]) + far
                    total[where] = piece if total[where] is None else total[where] + piece
        return total

    def total_middle(part, values, received):
        sided, taker, _ = table(part)
        total = None
        for a in range(3):
            inside, _, local, _ = sided[a]
            _, outside, _, off = taker[a]
            piece = rows_of(values[0] + jnp.where(inside, lanes_of(values[0], local), 0.0), flips[a])
            piece = piece + jnp.where(outside, lanes_of(rows_of(received, flips[a]), off), 0.0)
            total = piece if total is None else total + piece
        return [total]

    def total_coarse(part, values, received):
        inside, outside, local, off = table(part)[2]
        piece = jnp.where(inside, lanes_of(values[0], local), 0.0)
        piece = piece + jnp.where(outside, lanes_of(received, off), 0.0)
        return [jnp.broadcast_to(piece.sum(axis=0, keepdims=True), tile)]

    totals = (total_fine, total_middle, total_coarse)

    def total(depth, values, reach, rims=None):
        rims = dict(rims or {})
        for j in values:
            if abs(j) <= reach + 1:
                rims[j] = packed(j, values[j])
        result = {}
        for j in range(-reach, reach + 1):
            lower, upper = rims.get(j - 1), rims.get(j + 1)
            received = upper if lower is None else lower if upper is None else jnp.where(lane < half, lower, upper)
            result[j] = totals[depth](j, values[j], received)
        return result

    def sweep(depth, values, forcing, weight, reach, rims=None):
        found = total(depth, values, reach, rims)
        return {
            j: [(1.0 - OMEGA) * v + w * (f + t) for v, f, w, t in zip(values[j], forcing[j], weight[j], found[j])]
            for j in found
        }

    def defect_of(depth, values, forcing, screening, reach):
        found = total(depth, values, reach)
        return {
            j: masked(j, [f - ((6.0 + s) * v - t) for v, f, s, t in zip(values[j], forcing[j], screening[j], found[j])])
            for j in found
        }

    def weights(screening):
        return {j: masked(j, [OMEGA / (6.0 + s) for s in values]) for j, values in screening.items()}

    def start(forcing, weight):
        return {j: [w * f for w, f in zip(weight[j], forcing[j])] for j in forcing}

    def restrict_fine(values):
        result = jnp.broadcast_to(values[0].sum(axis=0, keepdims=True), tile)
        for j in range(1, 8):
            result = jnp.where(sub == j, values[j].sum(axis=0, keepdims=True), result)
        return [result * 0.5]

    def restrict_middle(values):
        return [jnp.broadcast_to(values[0].sum(axis=0, keepdims=True) * 0.5, tile)]

    for j in (-1, 1):
        for k, field in enumerate((current, forcing, screening)):
            arrive["near", j, k].wait_recv()
            field[j] = masked(j, load(near, place(j, 1), k))
    weight0, forcing0 = weights(screening), forcing
    rims = {}
    for j in (-2, 2):
        arrive["rim", j].wait_recv()
        rims[j] = rim[place(j, 2) // 3]
    current = sweep(0, current, forcing, weight0, 1, rims)
    kept0 = sweep(0, current, forcing, weight0, 1)
    for j in range(8):
        fine_out[j] = kept0[0][j]
    for o in offsets(1):
        arrive["fine", -o] = send(fine_out, fine.at[place(-o, 1)], o)
    defect = defect_of(0, kept0, forcing, screening, 0)
    kept0 = {0: kept0[0]}
    forcing1, screening1 = {0: restrict_fine(defect[0])}, {0: restrict_fine(screening[0])}

    middle_out[0] = forcing1[0][0]
    middle_out[1] = screening1[0][0]
    for o in offsets(REACH):
        arrive["middle", -o] = send(middle_out, middle.at[place(-o, REACH)], o)
    for j in offsets(REACH):
        table(j)
        arrive["middle", j].wait_recv()
        forcing1[j] = [middle[place(j, REACH), 0]]
        screening1[j] = [middle[place(j, REACH), 1]]
    weight1 = weights(screening1)
    kept1 = sweep(1, start(forcing1, weight1), forcing1, weight1, 2)
    forcing2 = {j: restrict_middle(v) for j, v in defect_of(1, kept1, forcing1, screening1, 1).items()}
    screening2 = {j: restrict_middle(v) for j, v in screening1.items()}
    weight2 = weights(screening2)
    kept2 = sweep(2, start(forcing2, weight2), forcing2, weight2, 1)
    grouped = defect_of(2, kept2, forcing2, screening2, 0)[0][0]
    for distance in (1, 2, 4):
        grouped = grouped + lanes_of(grouped, lane ^ distance)

    sums[rank] = grouped[0:1, :] * 0.5
    for k, value in enumerate((kept1, kept2, forcing2)):
        coarse_out[k] = value[0][0]
    arrived = [send(sums.at[rank], sums.at[rank], o) for o in range(1, devices)]
    for o in offsets(REACH):
        arrive["coarse", -o] = send(coarse_out, coarse.at[place(-o, REACH)], o)
    kept1, kept2, forcing2 = {0: kept1[0]}, {0: kept2[0]}, {0: forcing2[0]}
    for copy in arrived:
        copy.wait_recv()
    width, base, bases = devices, 0, []
    row = [sums[d] for d in range(devices)]
    while width > 1:
        width //= 2
        row = [row[2 * i] + row[2 * i + 1] for i in range(width)]
        bases.append(base)
        for i in range(width):
            tree[base + i] = row[i]
        base += width

    current = {}
    for j in [0] + offsets(REACH):
        if j:
            arrive["coarse", j].wait_recv()
            for k, field in enumerate((kept1, kept2, forcing2)):
                field[j] = [coarse[place(j, REACH), k]]
        other = at(j)
        correction = sums[other] / COARSE
        for k, base in enumerate(bases, 1):
            correction = correction + tree[base + other // 2**k] / (COARSE * 2**k)
        current[j] = [kept2[j][0] + jnp.where(live[j], jnp.broadcast_to(correction, tile), 0.0)]
    current = sweep(2, current, forcing2, weight2, 3)
    current = sweep(2, current, forcing2, weight2, 2)
    current = {j: [kept1[j][0] + masked(j, v)[0]] for j, v in current.items()}
    current = sweep(1, current, forcing1, weight1, 2)
    current = sweep(1, current, forcing1, weight1, 1)
    for j in (-1, 1):
        arrive["fine", j].wait_recv()
        kept0[j] = [fine[place(j, 1), k] for k in range(8)]
    current = {
        j: [a + jnp.where(live[j], jnp.broadcast_to(v[0][k : k + 1, :], tile), 0.0) for k, a in enumerate(kept0[j])]
        for j, v in current.items()
    }
    current = sweep(0, current, forcing0, weight0, 1)
    current = sweep(0, current, forcing0, weight0, 0)[0]

    spread = (sub & 1) + (sub >> 2) * 2
    upper = (sub & 2) != 0
    for hx in range(2):
        for hy in range(2):
            low, high = current[4 * hx + 2 * hy], current[4 * hx + 2 * hy + 1]
            for bx in range(2):
                row = 8 * (4 * hx + 2 * bx + hy)
                index = spread + 4 * bx
                out[row : row + 8, :] = jnp.where(upper, rows_of(high, index), rows_of(low, index))
    for copy in copies:
        copy.wait_send()


def per_device(rhs, screen, guess, counts, neighbours):
    shape = rhs.shape
    slots = shape[3]
    devices = lax.axis_size("sfc")
    rows = shape[0] * shape[1] * shape[2]
    vmem = pl.BlockSpec(memory_space=pltpu.VMEM)
    result = pl.pallas_call(
        lambda *refs: cycle_kernel(devices, slots, *refs),
        out_shape=jax.ShapeDtypeStruct((rows, slots), jnp.float32),
        in_specs=[pl.BlockSpec(memory_space=pltpu.SMEM)] + [vmem] * 4,
        out_specs=vmem,
        scratch_shapes=[
            pltpu.VMEM((2, 3, rows, slots), jnp.float32),
            pltpu.VMEM((2, 8, slots), jnp.float32),
            pltpu.VMEM((2 * REACH, *neighbours.shape), jnp.int32),
            pltpu.VMEM((2 * REACH, 2, 8, slots), jnp.float32),
            pltpu.VMEM((2, 8, 8, slots), jnp.float32),
            pltpu.VMEM((2 * REACH, 3, 8, slots), jnp.float32),
            pltpu.VMEM((devices, 1, slots), jnp.float32),
            pltpu.VMEM((devices, 1, slots), jnp.float32),
            pltpu.VMEM((8, slots), jnp.float32),
            pltpu.VMEM((2, 8, slots), jnp.float32),
            pltpu.VMEM((8, 8, slots), jnp.float32),
            pltpu.VMEM((3, 8, slots), jnp.float32),
            pltpu.SemaphoreType.DMA((10 + 6 * REACH + devices - 1,)),
            pltpu.SemaphoreType.DMA((10 + 6 * REACH + devices - 1,)),
        ],
        compiler_params=pltpu.CompilerParams(collective_id=0, has_side_effects=True),
        name="cycle",
    )(counts, rhs.reshape(rows, slots), screen.reshape(rows, slots), guess.reshape(rows, slots), neighbours)
    return result.reshape(shape)


def solution(mesh):
    blocks = P(None, None, None, "sfc")
    return jax.shard_map(
        per_device,
        mesh=mesh,
        in_specs=(blocks, blocks, blocks, P(), P(None, "sfc")),
        out_specs=blocks,
        check_vma=False,
    )
```

time: 237 us -> 26.7 us (0.11)
  the two profiles are of different devices: /device:TPU:15 before, /device:TPU:0 now
where the time goes in v2:
time: 26.7 us; the launch traced here: 26.5 us
  Pallas kernels  25.1 us (94%)
  local copies, waits for them, and re-layouts  1.38 us (5%)
    pallas_call x1, Pallas kernels, per_device(): pl.pallas_call(lambda *refs: cycle_kernel(devices, slots, *refs), out_sha...  25.1 us
    unnamed x1, local copies, waits for them, and re-layouts  1.38 us

profile of v2, /device:TPU:0, one launch (start us, length us, event | category | flops | bytes accessed | tf_op | source)
XLA Modules:
  0.0 26.5 jit_solution(7489578748304776559)
XLA Ops:
  0.0 25.1 %cycle.1 = f32[64,128]{1,0:T(8,128)} custom-call(s32[32]{0:T(128)} %refs_0_.1, f32[64,128]{1,0:T(8,128)} %bitcast.5, f32[64,128]{1,0:T(8,128)} %bitcast.6, f32[64,128]{1,0:T(8,128)} %bitcast.7, s32[6,128]{1,0:T(8,128)} %refs_4_.1), custom_call_target="tpu_custom_call" | custom-call | tf_op jit(solution)/shard_map/cycle/pallas_call | solution.py:319
  25.1 1.4 %copy.7 = f32[4,4,4,128]{3,2,1,0:T(4,128)} copy(f32[4,4,4,128]{3,2,1,0:T(4,128)} %bitcast.4) | data formatting | bytes 65536

commit v3 on v2

--- a/solution.py
+++ b/solution.py
@@ -21,14 +21,20 @@
 
 
 def cycle_kernel(
-    devices, slots, counts, rhs, screen, guess, neighbours, out,
+    devices, slots, counts, rhs_in, screen_in, guess_in, neighbours_in, out,
     near, rim, codes, middle, fine, coarse, sums, tree,
-    rim_out, middle_out, fine_out, coarse_out, send_sem, recv_sem,
+    rim_out, middle_out, fine_out, coarse_out, own, neighbours, send_sem, recv_sem, load_sem,
 ):
     rank = lax.axis_index("sfc")
 
     def at(offset):
         return lax.rem(rank + offset + devices, devices)
+
+    guess, rhs, screen = own.at[0], own.at[1], own.at[2]
+    pairs = ((guess_in, guess), (rhs_in, rhs), (screen_in, screen), (neighbours_in, neighbours))
+    loads = [pltpu.make_async_copy(a, b, load_sem.at[k]) for k, (a, b) in enumerate(pairs)]
+    for copy in loads:
+        copy.start()
 
     barrier = pltpu.get_barrier_semaphore()
     for offset in range(1, devices):
@@ -51,7 +57,20 @@
 
     copies = []
 
-    def send(source, target, offset):
+    def reaches(offset):
+        return rank < devices - offset if offset > 0 else rank >= -offset
+
+    class Arrival:
+        def __init__(self, copy, offset):
+            self.copy, self.offset = copy, offset
+
+        def wait_recv(self):
+            if self.offset:
+                pl.when(reaches(-self.offset))(self.copy.wait_recv)
+            else:
+                self.copy.wait_recv()
+
+    def send(source, target, offset, wrap=False):
         number = len(copies)
         copy = pltpu.make_async_remote_copy(
             src_ref=source,
@@ -61,9 +80,12 @@
             device_id=(at(offset),),
             device_id_type=MESH,
         )
-        copy.start()
-        copies.append(copy)
-        return copy
+        if wrap:
+            copy.start()
+        else:
+            pl.when(reaches(offset))(copy.start)
+        copies.append((copy, 0 if wrap else offset))
+        return Arrival(copy, 0 if wrap else offset)
 
     def place(offset, reach):
         return offset + reach if offset < 0 else offset + reach - 1
@@ -94,16 +116,19 @@
             result = jnp.where(pack_place == j, lanes_of(values[j], pack_index[part]), result)
         return result
 
-    forcing, screening, current = ({0: masked(0, load(r))} for r in (rhs, screen, guess))
-    rim_out[...] = packed(0, current[0])
+    for copy in loads:
+        copy.wait()
     pl.semaphore_wait(barrier, devices - 1)
     arrive = {}
-    for o in offsets(2)[2:]:
-        arrive["rim", -o] = send(rim_out, rim.at[place(-o, 2) // 3], o)
     for o in offsets(1):
         for k, ref in enumerate((guess, rhs, screen)):
             arrive["near", -o, k] = send(ref, near.at[place(-o, 1), k], o)
-    for o in offsets(REACH):
+        arrive["codes", -o] = send(neighbours, codes.at[place(-o, REACH)], o)
+    forcing, screening, current = ({0: masked(0, load(r))} for r in (rhs, screen, guess))
+    rim_out[...] = packed(0, current[0])
+    for o in offsets(2)[2:]:
+        arrive["rim", -o] = send(rim_out, rim.at[place(-o, 2) // 3], o)
+    for o in offsets(REACH)[2:]:
         arrive["codes", -o] = send(neighbours, codes.at[place(-o, REACH)], o)
 
     def decoded(part, code):
@@ -255,7 +280,7 @@
     sums[rank] = grouped[0:1, :] * 0.5
     for k, value in enumerate((kept1, kept2, forcing2)):
         coarse_out[k] = value[0][0]
-    arrived = [send(sums.at[rank], sums.at[rank], o) for o in range(1, devices)]
+    arrived = [send(sums.at[rank], sums.at[rank], o, True) for o in range(1, devices)]
     for o in offsets(REACH):
         arrive["coarse", -o] = send(coarse_out, coarse.at[place(-o, REACH)], o)
     kept1, kept2, forcing2 = {0: kept1[0]}, {0: kept2[0]}, {0: forcing2[0]}
@@ -306,8 +331,11 @@
                 row = 8 * (4 * hx + 2 * bx + hy)
                 index = spread + 4 * bx
                 out[row : row + 8, :] = jnp.where(upper, rows_of(high, index), rows_of(low, index))
-    for copy in copies:
-        copy.wait_send()
+    for copy, offset in copies:
+        if offset:
+            pl.when(reaches(offset))(copy.wait_send)
+        else:
+            copy.wait_send()
 
 
 def per_device(rhs, screen, guess, counts, neighbours):
@@ -319,7 +347,7 @@
     result = pl.pallas_call(
         lambda *refs: cycle_kernel(devices, slots, *refs),
         out_shape=jax.ShapeDtypeStruct((rows, slots), jnp.float32),
-        in_specs=[pl.BlockSpec(memory_space=pltpu.SMEM)] + [vmem] * 4,
+        in_specs=[pl.BlockSpec(memory_space=pltpu.SMEM)] + [pl.BlockSpec(memory_space=pl.ANY)] * 4,
         out_specs=vmem,
         scratch_shapes=[
             pltpu.VMEM((2, 3, rows, slots), jnp.float32),
@@ -334,8 +362,11 @@
             pltpu.VMEM((2, 8, slots), jnp.float32),
             pltpu.VMEM((8, 8, slots), jnp.float32),
             pltpu.VMEM((3, 8, slots), jnp.float32),
+            pltpu.VMEM((3, rows, slots), jnp.float32),
+            pltpu.VMEM(neighbours.shape, jnp.int32),
             pltpu.SemaphoreType.DMA((10 + 6 * REACH + devices - 1,)),
             pltpu.SemaphoreType.DMA((10 + 6 * REACH + devices - 1,)),
+            pltpu.SemaphoreType.DMA((4,)),
         ],
         compiler_params=pltpu.CompilerParams(collective_id=0, has_side_effects=True),
         name="cycle",

time: 26.7 us -> 24.9 us (0.933)
  Pallas kernels: 25.1 us -> 23.3 us
    pallas_call x1, Pallas kernels: 25.1 us -> 23.3 us  [per_device(): pl.pallas_call(lambda *refs: cycle_kernel(devices, slots, *refs), out_sha...]
where the time goes in v3:
time: 24.9 us; the launch traced here: 24.7 us
  Pallas kernels  23.3 us (94%)
  local copies, waits for them, and re-layouts  1.38 us (6%)
    pallas_call x1, Pallas kernels, per_device(): pl.pallas_call(lambda *refs: cycle_kernel(devices, slots, *refs), out_sha...  23.3 us
    unnamed x1, local copies, waits for them, and re-layouts  1.38 us

profile of v3, /device:TPU:0, one launch (start us, length us, event | category | flops | bytes accessed | tf_op | source)
XLA Modules:
  0.0 24.7 jit_solution(5494862170605312028)
XLA Ops:
  0.0 23.3 %cycle.1 = f32[64,128]{1,0:T(8,128)} custom-call(s32[32]{0:T(128)} %refs_0_.1, f32[64,128]{1,0:T(8,128)} %bitcast.5, f32[64,128]{1,0:T(8,128)} %bitcast.6, f32[64,128]{1,0:T(8,128)} %bitcast.7, s32[6,128]{1,0:T(8,128)} %refs_4_.1), custom_call_target="tpu_custom_call" | custom-call | tf_op jit(solution)/shard_map/cycle/pallas_call | solution.py:347
  23.3 1.4 %copy.7 = f32[4,4,4,128]{3,2,1,0:T(4,128)} copy(f32[4,4,4,128]{3,2,1,0:T(4,128)} %bitcast.4) | data formatting | bytes 65536

commit v4 on v3

--- a/solution.py
+++ b/solution.py
@@ -128,8 +128,6 @@
     rim_out[...] = packed(0, current[0])
     for o in offsets(2)[2:]:
         arrive["rim", -o] = send(rim_out, rim.at[place(-o, 2) // 3], o)
-    for o in offsets(REACH)[2:]:
-        arrive["codes", -o] = send(neighbours, codes.at[place(-o, REACH)], o)
 
     def decoded(part, code):
         inside = (code >= slots) & (code < 2 * slots)
@@ -198,20 +196,20 @@
 
     totals = (total_fine, total_middle, total_coarse)
 
-    def total(depth, values, reach, rims=None):
+    def total(depth, values, reach, rims=None, parts=None):
         rims = dict(rims or {})
         for j in values:
             if abs(j) <= reach + 1:
                 rims[j] = packed(j, values[j])
         result = {}
-        for j in range(-reach, reach + 1):
+        for j in parts or range(-reach, reach + 1):
             lower, upper = rims.get(j - 1), rims.get(j + 1)
             received = upper if lower is None else lower if upper is None else jnp.where(lane < half, lower, upper)
             result[j] = totals[depth](j, values[j], received)
         return result
 
-    def sweep(depth, values, forcing, weight, reach, rims=None):
-        found = total(depth, values, reach, rims)
+    def sweep(depth, values, forcing, weight, reach, rims=None, parts=None):
+        found = total(depth, values, reach, rims, parts)
         return {
             j: [(1.0 - OMEGA) * v + w * (f + t) for v, f, w, t in zip(values[j], forcing[j], weight[j], found[j])]
             for j in found
@@ -239,8 +237,15 @@
     def restrict_middle(values):
         return [jnp.broadcast_to(values[0].sum(axis=0, keepdims=True) * 0.5, tile)]
 
+    own_weight = weights(screening)
     for j in (-1, 1):
-        for k, field in enumerate((current, forcing, screening)):
+        arrive["near", j, 0].wait_recv()
+        current[j] = masked(j, load(near, place(j, 1), 0))
+    swept = sweep(0, current, forcing, own_weight, 0)
+    for o in offsets(REACH)[2:]:
+        arrive["codes", -o] = send(neighbours, codes.at[place(-o, REACH)], o)
+    for j in (-1, 1):
+        for k, field in ((1, forcing), (2, screening)):
             arrive["near", j, k].wait_recv()
             field[j] = masked(j, load(near, place(j, 1), k))
     weight0, forcing0 = weights(screening), forcing
@@ -248,12 +253,10 @@
     for j in (-2, 2):
         arrive["rim", j].wait_recv()
         rims[j] = rim[place(j, 2) // 3]
-    current = sweep(0, current, forcing, weight0, 1, rims)
+    current = {**swept, **sweep(0, current, forcing, weight0, 1, rims, (-1, 1))}
     kept0 = sweep(0, current, forcing, weight0, 1)
     for j in range(8):
         fine_out[j] = kept0[0][j]
-    for o in offsets(1):
-        arrive["fine", -o] = send(fine_out, fine.at[place(-o, 1)], o)
     defect = defect_of(0, kept0, forcing, screening, 0)
     kept0 = {0: kept0[0]}
     forcing1, screening1 = {0: restrict_fine(defect[0])}, {0: restrict_fine(screening[0])}
@@ -262,6 +265,8 @@
     middle_out[1] = screening1[0][0]
     for o in offsets(REACH):
         arrive["middle", -o] = send(middle_out, middle.at[place(-o, REACH)], o)
+    for o in offsets(1):
+        arrive["fine", -o] = send(fine_out, fine.at[place(-o, 1)], o)
     for j in offsets(REACH):
         table(j)
         arrive["middle", j].wait_recv()

time: 24.9 us -> 24.4 us (0.980)
  Pallas kernels: 23.3 us -> 22.7 us
    pallas_call x1, Pallas kernels: 23.3 us -> 22.7 us  [per_device(): pl.pallas_call(lambda *refs: cycle_kernel(devices, slots, *refs), out_sha...]
where the time goes in v4:
time: 24.4 us; the launch traced here: 24.1 us
  Pallas kernels  22.7 us (93%)
  local copies, waits for them, and re-layouts  1.38 us (6%)
    pallas_call x1, Pallas kernels, per_device(): pl.pallas_call(lambda *refs: cycle_kernel(devices, slots, *refs), out_sha...  22.7 us
    unnamed x1, local copies, waits for them, and re-layouts  1.38 us

profile of v4, /device:TPU:0, one launch (start us, length us, event | category | flops | bytes accessed | tf_op | source)
XLA Modules:
  0.0 24.1 jit_solution(4591594724872588405)
XLA Ops:
  0.0 22.7 %cycle.1 = f32[64,128]{1,0:T(8,128)} custom-call(s32[32]{0:T(128)} %refs_0_.1, f32[64,128]{1,0:T(8,128)} %bitcast.5, f32[64,128]{1,0:T(8,128)} %bitcast.6, f32[64,128]{1,0:T(8,128)} %bitcast.7, s32[6,128]{1,0:T(8,128)} %refs_4_.1), custom_call_target="tpu_custom_call" | custom-call | tf_op jit(solution)/shard_map/cycle/pallas_call | solution.py:352
  22.8 1.4 %copy.7 = f32[4,4,4,128]{3,2,1,0:T(4,128)} copy(f32[4,4,4,128]{3,2,1,0:T(4,128)} %bitcast.4) | data formatting | bytes 65536
